TPU v7x, 512 devices: a whole 4x8x8 slice. The times are simulated.
512 devices in a mesh: dp: 64 (over z, x, core), mp: 8 (over y).
Axes of the slice: x: 4, y: 8, z: 8, core: 2. Of those that a mesh axis runs over, the one named last changes fastest.
Arguments:
- teacher_in: bfloat16 [64, 1024, 1408], P('dp', 'mp'), may hold values from -8 to 8
- teacher_gain: float32 [1408], replicated, may hold values from 0.5 to 1.5
- teacher_qkv: bfloat16 [3, 1408, 1408], P(None, 'mp'), may hold values from -1 to 1
- teacher_out: bfloat16 [1408, 1408], P('mp'), may hold values from -0.15625 to 0.15625
- student_in: bfloat16 [64, 1024, 1024], P('dp', None, 'mp'), may hold values from -6 to 6
- student_gain: float32 [1024], replicated, may hold values from 0.25 to 1.75
- widen_weight: bfloat16 [1024, 4096], P(None, 'mp'), may hold values from -0.1875 to 0.1875
- narrow_weight: bfloat16 [4096, 1024], P('mp'), may hold values from -0.09375 to 0.09375
- target_head: bfloat16 [1408, 1024], P('mp'), may hold values from -0.1875 to 0.1875
- positions: int32 [64, 512], P('dp'), may hold values from 0 to 1023, as said below
- counts: int32 [64], P('dp'), may hold values from 1 to 512, 16384 in all
Outputs:
- grad_widen: float32 [1024, 4096], P('dp', 'mp')
- grad_narrow: float32 [1024, 4096], P('dp', 'mp')
- losses: float32 [64], P('dp')
Inputs may be any that keep to these rules, and one draw needn't show every extreme that they name: `positions`: the entries of one image's list are distinct; only the first counts of them are live. The counts of all images sum to 16384.
All inputs are finite; a program needn't handle non-finite values. No bound on the sum of `counts` on one device may be relied on, other than what follows from the above.
Results may differ from a plain program's by a relative error of at most 0.02.
Values may be sent and summed in bfloat16 or wider, within the bound.
No kernel may reach another device: no remote copies, remote signals or barrier semaphores. Data moves between devices by JAX's collectives and lax.ppermute only.
A program may use at most 64 MiB of HBM per device.

v0:
```python
import jax
import jax.numpy as jnp
from jax import lax
from jax.sharding import PartitionSpec as P

TD = 1408
TH = 16
EPSILON = 1e-06


def in_order(tiles, dim):
    tiles = jnp.moveaxis(tiles, 0, dim)
    dims = tiles.shape
    return tiles.reshape(*dims[:dim], dims[dim] * dims[dim + 1], *dims[dim + 2 :])


def sent_to_all(array, axis):
    copies = jnp.broadcast_to(array, (lax.axis_size(axis), *array.shape))
    return lax.all_to_all(copies, axis, split_axis=0, concat_axis=0, tiled=True)


def gather_directly(array, axis, dim):
    return in_order(sent_to_all(array, axis), dim)


def rows_for(lines, peers):
    spare = -lines.shape[0] % peers
    if not spare:
        return lines
    return jnp.concatenate([lines, jnp.zeros((spare, *lines.shape[1:]), lines.dtype)])


def total_of(array, axis):
    lines = array.reshape(-1, *array.shape[1:][-1:])
    own = lax.psum_scatter(
        rows_for(lines, lax.axis_size(axis)), axis, scatter_dimension=0, tiled=True
    )
    whole = lax.all_gather(own, axis).reshape(-1, *lines.shape[1:])
    return lax.slice_in_dim(whole, 0, len(lines)).reshape(array.shape)


def of_everyone(array, axis):
    everything = sent_to_all(array, axis)
    return jnp.sum(everything, axis=0)


def packed_total(arrays, axis):
    ends = [0]
    for a in arrays:
        ends.append(ends[-1] + a.size)
    so_far = of_everyone(jnp.concatenate([a.ravel() for a in arrays]), axis)
    return tuple((so_far[b:e].reshape(a.shape) for a, b, e in zip(arrays, ends, ends[1:])))


def cut_along(array, dim, peers):
    dims = array.shape
    tiles = array.reshape(*dims[:dim], peers, dims[dim] // peers, *dims[dim + 1 :])
    return jnp.moveaxis(tiles, dim, 0)


def summed_on_arrival(array, axis, dim):
    peers = lax.axis_size(axis)
    tiles = lax.all_to_all(cut_along(array, dim, peers), axis, 0, 0, tiled=True)
    return jnp.sum(tiles, axis=0)


def layer_norm(values, gain):
    mean_val = jnp.mean(values, axis=-1, keepdims=True)
    centred = values - mean_val
    spread = jnp.mean(centred * centred, axis=-1, keepdims=True)
    return centred * lax.rsqrt(spread + EPSILON) * gain


def gelu_value(pre):
    return 0.5 * pre * (1.0 + lax.erf(pre * 0.7071067811865476))


def gelu_slope(pre):
    return 0.5 * (1.0 + lax.erf(pre * 0.7071067811865476)) + pre * 0.3989422804014327 * jnp.exp(
        -0.5 * pre * pre
    )


def on_device(
    teacher_in,
    teacher_gain,
    teacher_qkv,
    teacher_out,
    student_in,
    student_gain,
    widen_weight,
    narrow_weight,
    target_head,
    positions,
    counts,
):
    patches_local = teacher_in[0]
    slot_total = positions.shape[1]
    picked = positions[0]
    live_count = counts[0]
    head_size = TD // TH
    factor = head_size ** (-0.5)
    local_width = teacher_qkv.shape[1]
    local_heads = local_width // head_size
    gathered = lax.all_gather(patches_local, "mp", axis=0, tiled=True)
    teach_normed = layer_norm(gathered.astype(jnp.float32), teacher_gain).astype(jnp.bfloat16)
    key_rows = jnp.einsum(
        "pi,oi->po", teach_normed, teacher_qkv[1], preferred_element_type=jnp.float32
    ).astype(jnp.bfloat16)
    value_rows = jnp.einsum(
        "pi,oi->po", teach_normed, teacher_qkv[2], preferred_element_type=jnp.float32
    ).astype(jnp.bfloat16)
    query_rows = jnp.einsum(
        "pi,oi->po", teach_normed[picked], teacher_qkv[0], preferred_element_type=jnp.float32
    ).astype(jnp.bfloat16)
    query_heads = query_rows.reshape(slot_total, local_heads, head_size)
    key_heads = key_rows.reshape(-1, local_heads, head_size)
    value_heads = value_rows.reshape(-1, local_heads, head_size)
    scores = (
        jnp.einsum("shd,phd->hsp", query_heads, key_heads, preferred_element_type=jnp.float32)
        * factor
    )
    largest = jnp.max(scores, axis=-1, keepdims=True)
    soft_num = jnp.exp(scores - largest)
    soft_weights = (soft_num / jnp.sum(soft_num, axis=-1, keepdims=True)).astype(jnp.bfloat16)
    attended = jnp.einsum(
        "hsp,phd->shd", soft_weights, value_heads, preferred_element_type=jnp.float32
    )
    attended = attended.astype(jnp.bfloat16).reshape(slot_total, local_width)
    blended = jnp.einsum(
        "sw,ow->so",
        gather_directly(attended, "mp", 1),
        teacher_out,
        preferred_element_type=jnp.float32,
    )
    own_start = lax.axis_index("mp") * local_width
    residual_part = lax.dynamic_slice_in_dim(gathered[picked], own_start, local_width, 1)
    targets = (residual_part.astype(jnp.float32) + blended).astype(jnp.bfloat16)
    slot_ids = jnp.arange(slot_total, dtype=jnp.int32)
    row_weight = jnp.where(
        slot_ids < live_count, 1.0 / live_count.astype(jnp.float32), jnp.zeros((), jnp.float32)
    )
    student_rows = student_in[0][picked]
    student_full = gather_directly(student_rows, "mp", 1)
    student_f32 = student_full.astype(jnp.float32)
    normed_rows = layer_norm(student_f32, student_gain).astype(jnp.bfloat16)
    pre_act = jnp.dot(normed_rows, widen_weight, preferred_element_type=jnp.float32)
    activity = gelu_value(pre_act).astype(jnp.bfloat16)
    branch_sum = total_of(
        jnp.dot(activity, narrow_weight, preferred_element_type=jnp.float32).astype(jnp.bfloat16),
        "mp",
    ).astype(jnp.float32)
    outputs = (student_f32 + branch_sum).astype(jnp.bfloat16)
    predicted = jnp.einsum("rd,cd->rc", outputs, target_head, preferred_element_type=jnp.float32)
    targets32 = targets.astype(jnp.float32)
    inner_sum, pred_sq, target_sq = packed_total(
        (
            jnp.sum(predicted * targets32, axis=-1),
            jnp.sum(predicted * predicted, axis=-1),
            jnp.sum(targets32 * targets32, axis=-1),
        ),
        "mp",
    )
    inv_pred = lax.rsqrt(pred_sq + EPSILON)
    inv_target = lax.rsqrt(target_sq + EPSILON)
    cosine = inner_sum * inv_pred * inv_target
    row_loss = row_weight * (1.0 - cosine)
    pred_slope = (row_weight * cosine * inv_pred * inv_pred)[:, None] * predicted - (
        row_weight * inv_pred * inv_target
    )[:, None] * targets32
    pred_slope = pred_slope.astype(jnp.bfloat16)
    back_sum = lax.psum(
        jnp.einsum("rc,cd->rd", pred_slope, target_head, preferred_element_type=jnp.float32).astype(
            jnp.bfloat16
        ),
        "mp",
    )
    back_act = jnp.einsum("rd,hd->rh", back_sum, narrow_weight, preferred_element_type=jnp.float32)
    back_pre = (back_act * gelu_slope(pre_act)).astype(jnp.bfloat16)
    column_part = normed_rows
    grad_widen = summed_on_arrival(
        jnp.einsum("rd,rh->dh", column_part, back_pre, preferred_element_type=jnp.float32), "dp", 0
    )
    column_part = back_sum
    grad_narrow = summed_on_arrival(
        jnp.einsum("rd,rh->dh", column_part, activity, preferred_element_type=jnp.float32), "dp", 0
    )
    image_loss = jnp.sum(row_loss)
    return (grad_widen, grad_narrow, jnp.reshape(image_loss, (1,)))


def solution(mesh):
    placed = (
        P("dp", "mp", None),
        P(),
        P(None, "mp", None),
        P("mp", None),
        P("dp", None, "mp"),
        P(),
        P(None, "mp"),
        P("mp", None),
        P("mp", None),
        P("dp", None),
        P("dp"),
    )
    return jax.shard_map(
        on_device,
        mesh=mesh,
        in_specs=placed,
        out_specs=(P("dp", "mp"), P("dp", "mp"), P("dp")),
        check_vma=False,
    )
```

profile of v0, /device:TPU:2, one launch (start us, length us, event | category | flops | bytes accessed | tf_op | source)
XLA Modules:
  0.0 403.2 jit_solution(8823197058762961276)
XLA Ops:
  7.2 0.7 all-gather.7.cloned.1.call-update
  8.0 0.7 compare_select_fusion
  8.7 2.0 gather_fusion
  10.9 42.5 %all_to_all.26 = bf16[8,512,128]{1,2,0:T(8,128)(2,1)S(1)} all-to-all(bf16[8,512,128]{1,2,0:T(8,128)(2,1)S(1)} %broadcast_in_dim.14), channel_id=1, replica_groups=mesh['dp'=64,'mp'=8] {'mp'}, dimensions={0} | all-to-all | bytes 2097152 | tf_op jit(solution)/shard_map/all_to_all | solution.py:19
  53.6 0.3 fusion.10
  54.0 0.3 fusion.13
  54.3 0.3 copy-done.13
  54.6 1.7 multiply_convert_fusion
  56.4 0.8 copy-done.9
  57.2 1.7 convolution_convert_fusion.1
  58.9 13.3 %all-gather.7.cloned.1.call-done = bf16[1,1024,1408]{2,1,0:T(8,128)(2,1)} async-done(((bf16[1,128,1408]{2,1,0:T(8,128)(2,1)}), bf16[1,1024,1408]{2,1,0:T(8,128)(2,1)}) %all-gather.7.cloned.1.call-update) | async-done | bytes 2883600 | tf_op jit(solution)/shard_map/all_gather | solution.py:105
  72.1 2.4 convert_reduce_fusion
  74.6 0.2 copy-done.1
  74.8 0.9 fusion.3
  75.7 2.5 fusion.5
  78.2 5.5 %gather_fusion.2 = bf16[512,1408]{1,0:T(8,128)(2,1)S(1)} fusion(bf16[1024,1408]{1,0:T(8,128)(2,1)} %fusion.5, s32[1024]{0:T(1024)S(1)} %pad_clamp_fusion), kind=kCustom, calls=%fused_computation.2 | custom fusion | bytes 2885632 | tf_op jit(solution)/shard_map/gather | solution.py:114
  83.8 2.4 convolution_convert_fusion.4
  86.2 3.1 convolution_convert_fusion.2
  89.3 1.1 convolution_convert_fusion.3
  90.4 3.4 fusion.52
  93.8 3.0 fusion.21
  96.8 1.2 broadcast_in_dim.17
  98.1 4.2 %all-to-all-start.1 = ((bf16[8,512,176]{1,2,0:T(8,128)(2,1)}), bf16[8,512,176]{1,2,0:T(8,128)(2,1)S(1)}, u32[]{:S(2)}, u32[]{:S(2)}) async-start(bf16[8,512,176]{1,2,0:T(8,128)(2,1)} %broadcast_in_dim.17), calls=%async_computation.1 | async-start | bytes 2883584 | tf_op jit(solution)/shard_map/all_to_all | solution.py:19
  102.3 0.2 all-gather.5.cloned.1.call-start
  102.5 22.0 %reduce-scatter.4.cloned.1.call-done = bf16[64,1024]{1,0:T(8,128)(2,1)} async-done(((bf16[512,1024]{1,0:T(8,128)(2,1)}), bf16[64,1024]{1,0:T(8,128)(2,1)}) %reduce-scatter.4.cloned.1.call-update) | async-done | bytes 131088 | tf_op jit(solution)/shard_map/reduce_scatter | solution.py:35
  124.6 6.3 %gather_fusion.1 = bf16[512,1408]{1,0:T(8,128)(2,1)} fusion(bf16[1024,1408]{1,0:T(8,128)(2,1)} %bitcast.75, s32[1024]{0:T(1024)S(1)} %pad_clamp_fusion), kind=kCustom, calls=%fused_computation.1 | custom fusion | bytes 2885632 | tf_op jit(solution)/shard_map/gather | solution.py:137
  130.9 1.9 constant_dynamic-slice_fusion
  132.7 1.7 copy.42
  134.5 35.3 %all-gather.5.cloned.1.call-done = bf16[512,1024]{1,0:T(8,128)(2,1)} async-done(((bf16[64,1024]{1,0:T(8,128)(2,1)}), bf16[512,1024]{1,0:T(8,128)(2,1)}) %all-gather.5.cloned.1.call-update) | async-done | bytes 1048592 | tf_op jit(solution)/shard_map/all_gather | solution.py:38
  169.7 2.3 copy.36
  172.0 2.5 fusion.14
  174.5 1.6 fusion.20
  176.2 0.4 multiply_reduce_fusion.3
  176.6 0.3 copy-done.4
  176.9 0.6 broadcast_in_dim.18
  177.6 4.3 %all-to-all-start.2 = ((f32[8,1,1536]{2,1,0:T(1,128)}), f32[8,1,1536]{2,1,0:T(1,128)S(1)}, u32[]{:S(2)}, u32[]{:S(2)}) async-start(f32[8,1,1536]{2,1,0:T(1,128)} %broadcast_in_dim.18), calls=%async_computation.2 | async-start | bytes 98304 | tf_op jit(solution)/shard_map/all_to_all | solution.py:19
  182.6 7.5 %all-to-all-done.2 = f32[8,1,1536]{2,1,0:T(1,128)S(1)} async-done(((f32[8,1,1536]{2,1,0:T(1,128)}), f32[8,1,1536]{2,1,0:T(1,128)S(1)}, u32[]{:S(2)}, u32[]{:S(2)}) %all-to-all-start.2) | async-done | bytes 49184 | tf_op jit(solution)/shard_map/all_to_all | solution.py:19
  190.1 0.6 fusion.43
  190.8 2.5 convolution_convert_fusion
  193.3 77.6 %all-reduce.2.cloned.1.call-done = bf16[512,1024]{1,0:T(8,128)(2,1)} async-done(((bf16[512,1024]{1,0:T(8,128)(2,1)}), bf16[512,1024]{1,0:T(8,128)(2,1)}) %all-reduce.2.cloned.1.call-update) | async-done | bytes 1048592 | tf_op jit(solution)/shard_map/psum | solution.py:172
  270.9 4.4 %fusion.22 = f32[64,16,512]{2,1,0:T(8,128)} fusion(bf16[64,16,512]{2,1,0:T(8,128)(2,1)S(1)} %bitcast.78, bf16[512,1024]{1,0:T(8,128)(2,1)} %all-reduce.2.cloned.1.call-done, bf16[512,1024]{1,0:T(8,128)(2,1)S(1)} %copy-done, f32[512,512]{1,0:T(8,128)} %get-tuple-element.13), kind=kOutput, calls=%fused_computation.40 | convolution fusion | flops 1076363264 | bytes 6291456 | tf_op jit(solution)/shard_map/rd,rh->dh/dot_general | solution.py:182
  275.3 10.9 %all-to-all-start.3 = ((f32[64,16,512]{2,1,0:T(8,128)}), f32[64,16,512]{2,1,0:T(8,128)S(1)}, u32[]{:S(2)}, u32[]{:S(2)}) async-start(f32[64,16,512]{2,1,0:T(8,128)} %fusion.22), calls=%async_computation.3 | async-start | bytes 4194304 | tf_op jit(solution)/shard_map/all_to_all | solution.py:63
  286.3 3.4 fusion.53
  289.7 47.9 %all-to-all-done.3 = f32[64,16,512]{2,1,0:T(8,128)S(1)} async-done(((f32[64,16,512]{2,1,0:T(8,128)}), f32[64,16,512]{2,1,0:T(8,128)S(1)}, u32[]{:S(2)}, u32[]{:S(2)}) %all-to-all-start.3) | async-done | bytes 2097184 | tf_op jit(solution)/shard_map/all_to_all | solution.py:63
  337.5 5.6 %all-to-all-start.4 = ((f32[64,16,512]{2,1,0:T(8,128)}), f32[64,16,512]{2,1,0:T(8,128)}, u32[]{:S(2)}, u32[]{:S(2)}) async-start(f32[64,16,512]{2,1,0:T(8,128)} %bitcast.21), calls=%async_computation.4 | async-start | bytes 4194304 | tf_op jit(solution)/shard_map/all_to_all | solution.py:63
  343.2 0.8 reduce_sum.117
  343.9 50.4 %all-to-all-done.4 = f32[64,16,512]{2,1,0:T(8,128)} async-done(((f32[64,16,512]{2,1,0:T(8,128)}), f32[64,16,512]{2,1,0:T(8,128)}, u32[]{:S(2)}, u32[]{:S(2)}) %all-to-all-start.4) | async-done | bytes 2097184 | tf_op jit(solution)/shard_map/all_to_all | solution.py:63
  394.3 2.3 reduce_sum.118
  (44 shorter events, 0.7 us)
Async XLA Ops:
  7.2 50.0 %copy-start = (bf16[512,1024]{1,0:T(8,128)(2,1)S(1)}, bf16[512,1024]{1,0:T(8,128)(2,1)}, u32[]{:S(2)}) copy-start(bf16[512,1024]{1,0:T(8,128)(2,1)} %param.18) | copy-start | bytes 3145732
  7.2 65.0 %all-gather.7.cloned.1.call-start = ((), (), s32[]{:S(2)}) async-start(), calls=%async_computation.8 | async-start | bytes 3244032 | tf_op jit(solution)/shard_map/all_gather | solution.py:105
  7.9 116.6 %reduce-scatter.4.cloned.1.call-start = ((), (), s32[]{:S(2)}) async-start(), calls=%async_computation.9 | async-start | bytes 1179648 | tf_op jit(solution)/shard_map/reduce_scatter | solution.py:35
  10.9 43.1 %copy-start.11 = (f32[1024]{0:T(1024)S(1)}, f32[1024]{0:T(1024)}, u32[]{:S(2)}) copy-start(f32[1024]{0:T(1024)} %param.16) | copy-start | bytes 12292
  53.4 1.2 copy-start.13
  54.6 1.7 copy-start.7
  56.4 0.8 copy-start.9
  72.1 2.7 copy-start.1
  74.5 1.2 copy-start.10
  83.8 2.5 copy-start.12
  86.2 3.1 copy-start.2
  89.3 1.1 copy-start.14
  98.1 76.4 %all-to-all-start.1 = ((bf16[8,512,176]{1,2,0:T(8,128)(2,1)}), bf16[8,512,176]{1,2,0:T(8,128)(2,1)S(1)}, u32[]{:S(2)}, u32[]{:S(2)}) async-start(bf16[8,512,176]{1,2,0:T(8,128)(2,1)} %broadcast_in_dim.17), calls=%async_computation.1 | async-start | bytes 2883584 | tf_op jit(solution)/shard_map/all_to_all | solution.py:19
  102.3 67.4 %all-gather.5.cloned.1.call-start = ((), (), s32[]{:S(2)}) async-start(), calls=%async_computation.7 | async-start | bytes 1179648 | tf_op jit(solution)/shard_map/all_gather | solution.py:38
  174.5 1.6 copy-start.3
  174.5 1.6 copy-start.5
  176.2 0.8 copy-start.4
  176.2 14.6 %copy-start.6 = (bf16[176,1024]{1,0:T(8,128)(2,1)S(1)}, bf16[176,1024]{1,0:T(8,128)(2,1)}, u32[]{:S(2)}) copy-start(bf16[176,1024]{1,0:T(8,128)(2,1)} %param.19) | copy-start | bytes 1081348
  176.9 94.0 %copy-start.8 = (bf16[512,1024]{0,1:T(8,128)(2,1)S(1)}, bf16[512,1024]{0,1:T(8,128)(2,1)}, u32[]{:S(2)}) copy-start(bf16[512,1024]{0,1:T(8,128)(2,1)} %copy-done.7) | copy-start | bytes 3145732
  177.6 12.5 %all-to-all-start.2 = ((f32[8,1,1536]{2,1,0:T(1,128)}), f32[8,1,1536]{2,1,0:T(1,128)S(1)}, u32[]{:S(2)}, u32[]{:S(2)}) async-start(f32[8,1,1536]{2,1,0:T(1,128)} %broadcast_in_dim.18), calls=%async_computation.2 | async-start | bytes 98304 | tf_op jit(solution)/shard_map/all_to_all | solution.py:19
  181.9 89.0 %all-reduce.2.cloned.1.call-start = ((), (), s32[]{:S(2)}) async-start(), calls=%async_computation.6 | async-start | bytes 2097152 | tf_op jit(solution)/shard_map/psum | solution.py:172
  275.3 62.2 %all-to-all-start.3 = ((f32[64,16,512]{2,1,0:T(8,128)}), f32[64,16,512]{2,1,0:T(8,128)S(1)}, u32[]{:S(2)}, u32[]{:S(2)}) async-start(f32[64,16,512]{2,1,0:T(8,128)} %fusion.22), calls=%async_computation.3 | async-start | bytes 4194304 | tf_op jit(solution)/shard_map/all_to_all | solution.py:63
  337.5 56.8 %all-to-all-start.4 = ((f32[64,16,512]{2,1,0:T(8,128)}), f32[64,16,512]{2,1,0:T(8,128)}, u32[]{:S(2)}, u32[]{:S(2)}) async-start(f32[64,16,512]{2,1,0:T(8,128)} %bitcast.21), calls=%async_computation.4 | async-start | bytes 4194304 | tf_op jit(solution)/shard_map/all_to_all | solution.py:63
Sparse Core Ops, SparseCore 0:
  10.1 61.9 all-gather.6
  75.0 49.5 reduce-scatter.3
  126.6 43.0 all-gather.4
  193.4 77.4 all-reduce.1
where the time goes:
time: 404 us; the launch traced here: 403 us
  waiting for transfers between devices  255 us (63%)
  blocking collectives  42.5 us (11%)
  matrix products  28.7 us (7%)
  starting transfers between devices  25.4 us (6%)
  local copies, waits for them, and re-layouts  23.6 us (6%)
  between operations  14.7 us (4%)
  other arithmetic  13.6 us (3%)
    all_to_all x2, waiting for transfers between devices, summed_on_arrival(): tiles = lax.all_to_all(cut_along(array, dim, peers), axis, 0, 0, tiled=True)  98.3 us
    psum x1, waiting for transfers between devices, on_device(): lax.psum(jnp.einsum('rc,cd->rd', pred_slope, target_head, preferred_eleme...  77.6 us
    all_to_all x1, blocking collectives, sent_to_all(): return lax.all_to_all(copies, axis, split_axis=0, concat_axis=0, tiled=True)  42.5 us
    all_gather x1, waiting for transfers between devices, total_of(): whole = lax.all_gather(own, axis).reshape(-1, *lines.shape[1:])  35.3 us
    reduce_scatter x1, waiting for transfers between devices, total_of(): lax.psum_scatter(rows_for(lines, lax.axis_size(axis)), axis, scatter_dime...  22 us
    all_to_all x2, starting transfers between devices, summed_on_arrival(): tiles = lax.all_to_all(cut_along(array, dim, peers), axis, 0, 0, tiled=True)  16.5 us
    all_gather x1, waiting for transfers between devices, on_device(): gathered = lax.all_gather(patches_local, 'mp', axis=0, tiled=True)  13.3 us
    all_to_all x2, starting transfers between devices, sent_to_all(): return lax.all_to_all(copies, axis, split_axis=0, concat_axis=0, tiled=True)  8.57 us
  transfers between devices with their start and end apart: 8, of which 7 were waited for; matrix products, arithmetic and copies ran while one was open for 13% of the time, Pallas kernels for 0%

commit v1 on v0

--- a/solution.py
+++ b/solution.py
@@ -102,7 +102,11 @@
     factor = head_size ** (-0.5)
     local_width = teacher_qkv.shape[1]
     local_heads = local_width // head_size
-    gathered = lax.all_gather(patches_local, "mp", axis=0, tiled=True)
+    size = lax.axis_size("mp")
+    repeats = [size if d == 0 else 1 for d in range(patches_local.ndim)]
+    gathered = lax.all_to_all(
+        jnp.tile(patches_local, repeats), "mp", split_axis=0, concat_axis=0, tiled=True
+    )
     teach_normed = layer_norm(gathered.astype(jnp.float32), teacher_gain).astype(jnp.bfloat16)
     key_rows = jnp.einsum(
         "pi,oi->po", teach_normed, teacher_qkv[1], preferred_element_type=jnp.float32

time: 404 us -> 451 us (1.12)
  waiting for transfers between devices: 255 us -> 297 us
  other arithmetic: 13.6 us -> 22.3 us
  blocking collectives: 42.5 us -> 35.6 us
    all_to_all x0 -> x1, waiting for transfers between devices: none -> 71 us  [on_device(): lax.all_to_all(jnp.tile(patches_local, repeats), 'mp', split_axis=0, conc...]
    reduce_scatter x1, waiting for transfers between devices: 22 us -> 0.02 us  [total_of(): lax.psum_scatter(rows_for(lines, lax.axis_size(axis)), axis, scatter_dime...]
    all_gather x1 -> x0, waiting for transfers between devices: 13.3 us -> none  [on_device(): gathered = lax.all_gather(patches_local, 'mp', axis=0, tiled=True)]
    all_gather x1, waiting for transfers between devices: 35.3 us -> 42.9 us  [total_of(): whole = lax.all_gather(own, axis).reshape(-1, *lines.shape[1:])]
    all_to_all x1, blocking collectives: 42.5 us -> 35.6 us  [sent_to_all(): return lax.all_to_all(copies, axis, split_axis=0, concat_axis=0, tiled=True)]
    convert_element_type x1 -> x2, other arithmetic: 2.51 us -> 7.16 us  [on_device(): layer_norm(gathered.astype(jnp.float32), teacher_gain).astype(jnp.bfloat16)]
    all_to_all x0 -> x1, starting transfers between devices: none -> 4.55 us  [on_device(): lax.all_to_all(jnp.tile(patches_local, repeats), 'mp', split_axis=0, conc...]
  transfers between devices with their start and end apart: 8 -> 8, of which waited for: 7 -> 6; matrix products, arithmetic and copies ran while one was open for 13% -> 12% of each run, Pallas kernels for 0% -> 0%
where the time goes in v1:
time: 451 us; the launch traced here: 450 us
  waiting for transfers between devices  297 us (66%)
  blocking collectives  35.6 us (8%)
  starting transfers between devices  29.9 us (7%)
  matrix products  25.4 us (6%)
  local copies, waits for them, and re-layouts  24.7 us (5%)
  other arithmetic  22.3 us (5%)
  between operations  14.7 us (3%)
    all_to_all x2, waiting for transfers between devices, summed_on_arrival(): tiles = lax.all_to_all(cut_along(array, dim, peers), axis, 0, 0, tiled=True)  95.9 us
    psum x1, waiting for transfers between devices, on_device(): lax.psum(jnp.einsum('rc,cd->rd', pred_slope, target_head, preferred_eleme...  79.7 us
    all_to_all x1, waiting for transfers between devices, on_device(): lax.all_to_all(jnp.tile(patches_local, repeats), 'mp', split_axis=0, conc...  71 us
    all_gather x1, waiting for transfers between devices, total_of(): whole = lax.all_gather(own, axis).reshape(-1, *lines.shape[1:])  42.9 us
    all_to_all x1, blocking collectives, sent_to_all(): return lax.all_to_all(copies, axis, split_axis=0, concat_axis=0, tiled=True)  35.6 us
    all_to_all x2, starting transfers between devices, summed_on_arrival(): tiles = lax.all_to_all(cut_along(array, dim, peers), axis, 0, 0, tiled=True)  16.8 us
  transfers between devices with their start and end apart: 8, of which 6 were waited for; matrix products, arithmetic and copies ran while one was open for 12% of the time, Pallas kernels for 0%

profile of v1, /device:TPU:2, one launch (start us, length us, event | category | flops | bytes accessed | tf_op | source)
XLA Modules:
  0.0 450.1 jit_solution(14316512509708053271)
XLA Ops:
  7.2 0.8 compare_select_fusion
  8.0 2.0 gather_fusion
  10.2 35.6 %all_to_all.35 = bf16[8,512,128]{1,2,0:T(8,128)(2,1)S(1)} all-to-all(bf16[8,512,128]{1,2,0:T(8,128)(2,1)S(1)} %broadcast_in_dim.14), channel_id=1, replica_groups=mesh['dp'=64,'mp'=8] {'mp'}, dimensions={0} | all-to-all | bytes 2097152 | tf_op jit(solution)/shard_map/all_to_all | solution.py:19
  45.9 1.8 tile.9
  47.7 4.6 %all-to-all-start.1 = ((bf16[8,128,1408]{2,1,0:T(8,128)(2,1)}), bf16[8,128,1408]{2,1,0:T(8,128)(2,1)}, u32[]{:S(2)}, u32[]{:S(2)}) async-start(bf16[8,128,1408]{2,1,0:T(8,128)(2,1)} %tile.9), calls=%async_computation.1 | async-start | bytes 5767168 | tf_op jit(solution)/shard_map/all_to_all | solution.py:107
  52.5 0.3 fusion.10
  52.9 0.3 fusion.13
  53.2 0.3 copy-done.11
  53.5 1.7 multiply_convert_fusion.1
  55.2 0.8 copy-done.5
  56.0 1.7 convolution_convert_fusion.1
  57.7 71.0 %all-to-all-done.1 = bf16[8,128,1408]{2,1,0:T(8,128)(2,1)} async-done(((bf16[8,128,1408]{2,1,0:T(8,128)(2,1)}), bf16[8,128,1408]{2,1,0:T(8,128)(2,1)}, u32[]{:S(2)}, u32[]{:S(2)}) %all-to-all-start.1) | async-done | bytes 2883616 | tf_op jit(solution)/shard_map/all_to_all | solution.py:107
  128.7 2.3 convert_reduce_fusion
  130.9 2.7 fusion.3
  133.6 0.6 fusion.52
  134.2 4.3 multiply_convert_fusion
  138.6 5.5 %gather_fusion.2 = bf16[512,1408]{1,0:T(8,128)(2,1)S(1)} fusion(bf16[1024,1408]{1,0:T(8,128)(2,1)} %multiply_convert_fusion, s32[1024]{0:T(1024)S(1)} %pad_clamp_fusion), kind=kCustom, calls=%fused_computation.2 | custom fusion | bytes 2885632 | tf_op jit(solution)/shard_map/gather | solution.py:118
  144.1 2.8 fusion.5
  147.0 1.3 convolution_convert_fusion.4
  148.3 1.1 convolution_convert_fusion.2
  149.4 1.1 convolution_convert_fusion.3
  150.5 3.4 fusion.54
  153.8 3.0 fusion.21
  156.9 1.3 broadcast_in_dim.17
  158.1 3.6 all-to-all-start.2
  162.0 0.5 all-gather.3.cloned.1.call-update
  162.5 6.3 %gather_fusion.1 = bf16[512,1408]{1,0:T(8,128)(2,1)} fusion(bf16[1024,1408]{1,0:T(8,128)(2,1)} %bitcast.10, s32[1024]{0:T(1024)S(1)} %pad_clamp_fusion), kind=kCustom, calls=%fused_computation.1 | custom fusion | bytes 2885632 | tf_op jit(solution)/shard_map/gather | solution.py:141
  168.8 1.9 constant_dynamic-slice_fusion
  170.6 1.7 copy.42
  172.4 42.9 %all-gather.3.cloned.1.call-done = bf16[512,1024]{1,0:T(8,128)(2,1)} async-done(((bf16[64,1024]{1,0:T(8,128)(2,1)}), bf16[512,1024]{1,0:T(8,128)(2,1)}) %all-gather.3.cloned.1.call-update) | async-done | bytes 1048592 | tf_op jit(solution)/shard_map/all_gather | solution.py:38
  215.2 2.3 copy.36
  217.5 2.5 fusion.14
  220.0 1.6 fusion.20
  221.6 1.8 multiply_reduce_fusion.3
  223.4 0.6 broadcast_in_dim.18
  224.0 4.6 %all-to-all-start.3 = ((f32[8,1,1536]{2,1,0:T(1,128)}), f32[8,1,1536]{2,1,0:T(1,128)S(1)}, u32[]{:S(2)}, u32[]{:S(2)}) async-start(f32[8,1,1536]{2,1,0:T(1,128)} %broadcast_in_dim.18), calls=%async_computation.3 | async-start | bytes 98304 | tf_op jit(solution)/shard_map/all_to_all | solution.py:19
  229.4 7.5 %all-to-all-done.3 = f32[8,1,1536]{2,1,0:T(1,128)S(1)} async-done(((f32[8,1,1536]{2,1,0:T(1,128)}), f32[8,1,1536]{2,1,0:T(1,128)S(1)}, u32[]{:S(2)}, u32[]{:S(2)}) %all-to-all-start.3) | async-done | bytes 49184 | tf_op jit(solution)/shard_map/all_to_all | solution.py:19
  236.9 0.6 fusion.43
  237.5 1.5 convolution_convert_fusion
  239.0 79.7 %all-reduce.2.cloned.1.call-done = bf16[512,1024]{1,0:T(8,128)(2,1)} async-done(((bf16[512,1024]{1,0:T(8,128)(2,1)}), bf16[512,1024]{1,0:T(8,128)(2,1)}) %all-reduce.2.cloned.1.call-update) | async-done | bytes 1048592 | tf_op jit(solution)/shard_map/psum | solution.py:176
  318.7 3.3 fusion.55
  322.0 11.2 %all-to-all-start.5 = ((f32[64,16,512]{2,1,0:T(8,128)}), f32[64,16,512]{2,1,0:T(8,128)}, u32[]{:S(2)}, u32[]{:S(2)}) async-start(f32[64,16,512]{2,1,0:T(8,128)} %bitcast.79), calls=%async_computation.5 | async-start | bytes 4194304 | tf_op jit(solution)/shard_map/all_to_all | solution.py:63
  333.2 4.1 fusion.22
  337.3 47.1 %all-to-all-done.5 = f32[64,16,512]{2,1,0:T(8,128)} async-done(((f32[64,16,512]{2,1,0:T(8,128)}), f32[64,16,512]{2,1,0:T(8,128)}, u32[]{:S(2)}, u32[]{:S(2)}) %all-to-all-start.5) | async-done | bytes 2097184 | tf_op jit(solution)/shard_map/all_to_all | solution.py:63
  384.4 5.6 %all-to-all-start.4 = ((f32[64,16,512]{2,1,0:T(8,128)}), f32[64,16,512]{2,1,0:T(8,128)}, u32[]{:S(2)}, u32[]{:S(2)}) async-start(f32[64,16,512]{2,1,0:T(8,128)} %fusion.22), calls=%async_computation.4 | async-start | bytes 4194304 | tf_op jit(solution)/shard_map/all_to_all | solution.py:63
  390.0 2.3 reduce_sum.118
  392.4 48.8 %all-to-all-done.4 = f32[64,16,512]{2,1,0:T(8,128)} async-done(((f32[64,16,512]{2,1,0:T(8,128)}), f32[64,16,512]{2,1,0:T(8,128)}, u32[]{:S(2)}, u32[]{:S(2)}) %all-to-all-start.4) | async-done | bytes 2097184 | tf_op jit(solution)/shard_map/all_to_all | solution.py:63
  441.2 2.3 reduce_sum.117
  (41 shorter events, 0.9 us)
Async XLA Ops:
  7.2 48.8 %copy-start = (bf16[512,1024]{1,0:T(8,128)(2,1)S(1)}, bf16[512,1024]{1,0:T(8,128)(2,1)}, u32[]{:S(2)}) copy-start(bf16[512,1024]{1,0:T(8,128)(2,1)} %param.18) | copy-start | bytes 3145732
  7.2 38.7 %copy-start.7 = (bf16[1,128,1408]{2,1,0:T(8,128)(2,1)S(1)}, bf16[1,128,1408]{2,1,0:T(8,128)(2,1)}, u32[]{:S(2)}) copy-start(bf16[1,128,1408]{2,1,0:T(8,128)(2,1)} %param.11) | copy-start | bytes 1081348
  47.7 5.2 %copy-start.9 = (f32[1024]{0:T(1024)S(1)}, f32[1024]{0:T(1024)}, u32[]{:S(2)}) copy-start(f32[1024]{0:T(1024)} %param.16) | copy-start | bytes 12292
  47.7 81.0 %all-to-all-start.1 = ((bf16[8,128,1408]{2,1,0:T(8,128)(2,1)}), bf16[8,128,1408]{2,1,0:T(8,128)(2,1)}, u32[]{:S(2)}, u32[]{:S(2)}) async-start(bf16[8,128,1408]{2,1,0:T(8,128)(2,1)} %tile.9), calls=%async_computation.1 | async-start | bytes 5767168 | tf_op jit(solution)/shard_map/all_to_all | solution.py:107
  52.2 1.2 copy-start.11
  52.2 109.7 %reduce-scatter.4.cloned.1.call-start = ((), (), s32[]{:S(2)}) async-start(), calls=%async_computation.9 | async-start | bytes 1179648 | tf_op jit(solution)/shard_map/reduce_scatter | solution.py:35
  53.5 1.7 copy-start.3
  55.2 0.8 copy-start.5
  57.7 76.6 %copy-start.8 = (f32[1408]{0:T(1024)S(1)}, f32[1408]{0:T(1024)}, u32[]{:S(2)}) copy-start(f32[1408]{0:T(1024)} %param.12) | copy-start | bytes 16900
  144.1 2.9 copy-start.10
  149.4 1.1 copy-start.12
  158.1 61.9 %all-to-all-start.2 = ((bf16[8,512,176]{1,2,0:T(8,128)(2,1)}), bf16[8,512,176]{1,2,0:T(8,128)(2,1)S(1)}, u32[]{:S(2)}, u32[]{:S(2)}) async-start(bf16[8,512,176]{1,2,0:T(8,128)(2,1)} %broadcast_in_dim.17), calls=%async_computation.2 | async-start | bytes 2883584 | tf_op jit(solution)/shard_map/all_to_all | solution.py:19
  161.7 53.5 %all-gather.3.cloned.1.call-start = ((), (), s32[]{:S(2)}) async-start(), calls=%async_computation.8 | async-start | bytes 1179648 | tf_op jit(solution)/shard_map/all_gather | solution.py:38
  220.0 17.5 %copy-start.1 = (bf16[176,1024]{1,0:T(8,128)(2,1)S(1)}, bf16[176,1024]{1,0:T(8,128)(2,1)}, u32[]{:S(2)}) copy-start(bf16[176,1024]{1,0:T(8,128)(2,1)} %param.19) | copy-start | bytes 1081348
  221.6 97.1 %copy-start.6 = (bf16[512,512]{1,0:T(8,128)(2,1)S(1)}, bf16[512,512]{1,0:T(8,128)(2,1)}, u32[]{:S(2)}) copy-start(bf16[512,512]{1,0:T(8,128)(2,1)} %copy-done.5) | copy-start | bytes 1572868
  224.0 12.8 %all-to-all-start.3 = ((f32[8,1,1536]{2,1,0:T(1,128)}), f32[8,1,1536]{2,1,0:T(1,128)S(1)}, u32[]{:S(2)}, u32[]{:S(2)}) async-start(f32[8,1,1536]{2,1,0:T(1,128)} %broadcast_in_dim.18), calls=%async_computation.3 | async-start | bytes 98304 | tf_op jit(solution)/shard_map/all_to_all | solution.py:19
  228.6 90.1 %all-reduce.2.cloned.1.call-start = ((), (), s32[]{:S(2)}) async-start(), calls=%async_computation.7 | async-start | bytes 2097152 | tf_op jit(solution)/shard_map/psum | solution.py:176
  322.0 11.2 %copy-start.2 = (bf16[512,1024]{1,0:T(8,128)(2,1)S(1)}, bf16[512,1024]{1,0:T(8,128)(2,1)}, u32[]{:S(2)}) copy-start(bf16[512,1024]{1,0:T(8,128)(2,1)} %all-reduce.2.cloned.1.call-done) | copy-start | bytes 3145732
  322.0 11.2 %copy-start.4 = (bf16[512,1024]{0,1:T(8,128)(2,1)S(1)}, bf16[512,1024]{0,1:T(8,128)(2,1)}, u32[]{:S(2)}) copy-start(bf16[512,1024]{0,1:T(8,128)(2,1)} %copy-done.3) | copy-start | bytes 3145732
  322.0 62.4 %all-to-all-start.5 = ((f32[64,16,512]{2,1,0:T(8,128)}), f32[64,16,512]{2,1,0:T(8,128)}, u32[]{:S(2)}, u32[]{:S(2)}) async-start(f32[64,16,512]{2,1,0:T(8,128)} %bitcast.79), calls=%async_computation.5 | async-start | bytes 4194304 | tf_op jit(solution)/shard_map/all_to_all | solution.py:63
  384.4 56.8 %all-to-all-start.4 = ((f32[64,16,512]{2,1,0:T(8,128)}), f32[64,16,512]{2,1,0:T(8,128)}, u32[]{:S(2)}, u32[]{:S(2)}) async-start(f32[64,16,512]{2,1,0:T(8,128)} %fusion.22), calls=%async_computation.4 | async-start | bytes 4194304 | tf_op jit(solution)/shard_map/all_to_all | solution.py:63
Sparse Core Ops, SparseCore 0:
  57.8 59.2 reduce-scatter.3
  164.6 50.5 all-gather.2
  239.1 79.5 all-reduce.1
